TPU v7x, 32 devices: a whole 2x2x4 slice. The times are simulated.
32 devices in a mesh: wall: 4 (over z), span: 8 (over y, x, core).
Axes of the slice: x: 2, y: 2, z: 4, core: 2. Of those that a mesh axis runs over, the one named last changes fastest.
Arguments:
- velocity: float32 [3, 4, 1024, 1024], P(None, None, 'wall', 'span'), may hold values from -6 to 6
- lower_weight: float32 [4, 1024, 1024], P(None, 'wall', 'span'), may hold values from 1000 to 100000
- upper_weight: float32 [4, 1024, 1024], P(None, 'wall', 'span'), may hold values from 1000 to 100000
- forces: float32 [3, 4, 8, 8, 4, 768], P(None, 'wall', 'span'), may hold values from -6 to 6
- cells: int32 [4, 8, 8, 4, 768], P('wall', 'span'), may hold values from 0 to 32767
- counts: int32 [4, 8, 8, 4], P('wall', 'span'), may hold values from 1 to 768, as said below
Outputs:
- velocity_next: float32 [3, 4, 1024, 1024], P(None, None, 'wall', 'span')
- deposit: bfloat16 [3, 4, 1024, 1024], P(None, None, 'wall', 'span')
Inputs may be any that keep to these rules, and one draw needn't show every extreme that they name: `counts`: in every wall row one destination receives 768 live slots from every sender in one plane.
All inputs are finite; a program needn't handle non-finite values.
Results may differ from a plain program's by a relative error of at most 0.0024.
Values sent between devices are 32-bit elements; how exact they have to be, the bound alone decides.
No kernel may reach another device: no remote copies, remote signals or barrier semaphores. Data moves between devices by JAX's collectives and lax.ppermute only.
A program may use at most 64 MiB of HBM per device.

v0:
```python
import jax
import jax.numpy as jnp
from jax import lax
from jax.experimental import pallas as pl
from jax.experimental.pallas import tpu as pltpu
from jax.sharding import PartitionSpec as P

diffusion_number = 0.2
segments = 8
lanes = 128
group = 8
count_bits, plane_bit = 10, 24
in_vmem = pl.BlockSpec(memory_space=pltpu.VMEM)
in_smem = pl.BlockSpec(memory_space=pltpu.SMEM)
in_hbm = pl.BlockSpec(memory_space=pltpu.HBM)


def call(body, out_shape, out_specs, in_specs, scratch, mebibytes, flops):
    return pl.pallas_call(
        body,
        out_shape=out_shape,
        in_specs=in_specs,
        out_specs=out_specs,
        scratch_shapes=scratch,
        compiler_params=pltpu.CompilerParams(vmem_limit_bytes=mebibytes << 20),
        cost_estimate=pl.CostEstimate(flops=flops, bytes_accessed=4 << 20, transcendentals=0),
    )


def f32(*shape):
    return jax.ShapeDtypeStruct(shape, jnp.float32)


def scratch(*shape):
    return pltpu.VMEM(shape, jnp.float32)


def lane_iota(shape):
    return lax.broadcasted_iota(jnp.int32, shape, len(shape) - 1)


def reciprocal(value):
    rough = pl.reciprocal(value, approx=True)
    return rough * (2.0 - value * rough)


def start_all(copies):
    for copy in copies:
        copy.start()


def wait_all(copies):
    for copy in copies:
        copy.wait()


def copies_of(sources, targets, sems, first=0):
    return [
        pltpu.make_async_copy(source, target, sems.at[first + n])
        for n, (source, target) in enumerate(zip(sources, targets))
    ]


def load_kernel(forces, velocity, lower, upper, counts_hbm, send, *refs):
    near, work_out, (slots, counts, work, sems) = refs[:3], refs[3], refs[4:]
    components, senders, planes, capacity = forces.shape
    chunks = capacity // lanes
    sources = [counts_hbm] + [forces.at[c] for c in range(components)]
    targets = [counts] + [slots.at[c] for c in range(components)]
    sources += [lower, upper] + [velocity.at[c] for c in range(components)]
    targets += [near[0], near[1]] + [near[2].at[c] for c in range(components)]
    copies = copies_of(sources, targets, sems)
    start_all(copies)
    outgoing = copies_of(
        [slots.at[c] for c in range(components)] + [work],
        [send.at[:, c] for c in range(components)] + [work_out],
        sems,
        len(copies),
    )

    def one_plane(x, n):
        def one_sender(s, n):
            count = counts[x, s]
            base = (x << plane_bit) + ((s * chunks) << count_bits)
            for k in range(chunks):
                live = jnp.maximum(count - k * lanes, 0)
                work[group + n + k] = base + (k << count_bits) + live
            return n + lax.div(count + lanes - 1, lanes)

        n = lax.fori_loop(0, senders, one_sender, n, unroll=4)
        for extra in range(group):
            work[group + n + extra] = x << plane_bit
        return lax.div(n + group - 1, group) * group

    copies[0].wait()
    total = lax.fori_loop(0, planes // 2, one_plane, 0)
    for c in range(components):
        copies[1 + c].wait()
        outgoing[c].start()
    total = lax.fori_loop(planes // 2, planes, one_plane, total)
    for extra in range(2 * group):
        work[group + total + extra] = 0
    work[0] = lax.div(total, group)
    outgoing[components].start()
    wait_all(copies[1 + components :])
    wait_all(outgoing)


def edge_kernel(velocity, first_out, last_out, columns, turned):
    components, planes, height, across = velocity.shape
    lines = components * planes
    lane = lane_iota((height, across))
    picked = jnp.zeros((height, across), jnp.float32)
    for k in range(lines):
        rolled = pltpu.roll(velocity[k // planes, k % planes], 2 * k + 1, 1)
        picked = jnp.where((lane >> 1) == k, rolled, picked)
    columns[...] = picked
    for p in range(height // lanes):
        turned[p] = columns[p * lanes : (p + 1) * lanes, :].T
        part = slice(p * lines, (p + 1) * lines)
        first_out[part, :] = turned[p, pl.ds(1, lines, stride=2), :]
        last_out[part, :] = turned[p, pl.ds(0, lines, stride=2), :]


def prepare_kernel(velocity, lower, upper, inner, ends, coefs, *refs):
    (rhs, inv, first) = refs[3:6]
    (inv_b, gain_b, rows, sems) = refs[6:]
    outgoing = copies_of(refs[3:6], refs[:3], sems)
    components, planes, height, across = velocity.shape
    steps = inv.shape[0] + 1
    last = steps - 1
    rest = height - segments * steps
    knots = segments + rest

    def of_step(ref, t):
        return ref[:, pl.ds(t, segments, stride=steps), :]

    one = jnp.ones((planes, segments, across), jnp.float32)
    zero = jnp.zeros_like(one)
    size = 8
    lane = lane_iota((size, across))

    def stencil_rows(n):
        return pl.ds(pl.multiple_of(n * size, size), size)

    def read_rows(n):
        part = stencil_rows(n)
        return [[velocity[c, x, part, :] for x in range(planes)] for c in range(components)]

    def stencil(values):
        found = []
        for x in range(planes):
            v = values[x]
            around = values[(x - 1) % planes] + values[(x + 1) % planes]
            around = around + jnp.where(lane == 0, 0.0, pltpu.roll(v, 1, 1))
            around = around + jnp.where(lane == across - 1, 0.0, pltpu.roll(v, across - 1, 1))
            found.append((1.0 - 4.0 * diffusion_number) * v + diffusion_number * around)
        return found

    def write_rows(n, values):
        part = stencil_rows(n)
        for c in range(components):
            for x in range(planes):
                rhs[c, x, part, :] = values[c][x]

    def factor(t, carry):
        d, d_b, low_gain, high_gain, sum_last, sum_first = carry
        back = last - 1 - t
        low, up = of_step(lower, t), of_step(upper, t)
        low_b, up_b = of_step(lower, back), of_step(upper, back)
        velocities = read_rows(t)
        e = 1.0 + low * d
        inverse = reciprocal(up + e)
        g = low * inverse
        e_b = 1.0 + up_b * d_b
        inverse_b = reciprocal(low_b + e_b)
        g_b = up_b * inverse_b
        found = [stencil(values) for values in velocities]
        inv[t] = inverse
        inv_b[back] = inverse_b
        gain_b[back] = g_b
        write_rows(t, found)
        return (
            e * inverse,
            e_b * inverse_b,
            low_gain * g,
            high_gain * g_b,
            inverse + g * sum_last,
            inverse_b + g_b * sum_first,
        )

    carry = lax.fori_loop(0, last, factor, (one, one, one, one, zero, zero), unroll=2)
    _, _, low_gain, high_gain, sum_last, sum_first = carry
    for n in range(last, height // size):
        write_rows(n, [stencil(values) for values in read_rows(n)])
    start_all(outgoing[:2])
    def weigh(t, q):
        first[t] = inv_b[t] * q
        return q * gain_b[t]

    lax.fori_loop(0, last, weigh, one, unroll=6)
    outgoing[2].start()

    low_sep, up_sep = of_step(lower, last), of_step(upper, last)
    segment = lax.broadcasted_iota(jnp.int32, one.shape, 1)
    is_end = segment == segments - 1
    above = jnp.where(is_end, 0.0, jnp.roll(sum_first, -1, axis=1))
    couple_high = up_sep * jnp.where(is_end, 1.0, jnp.roll(high_gain, -1, axis=1))
    killing = 1.0 + low_sep * sum_last + up_sep * above
    ends[2, :, :segments, :] = low_sep
    ends[3, :, :segments, :] = up_sep
    tail = slice(height - rest, height)
    low_rest, up_rest = lower[:, tail, :], upper[:, tail, :]
    for n, (value, other) in enumerate(
        (
            (low_sep * low_gain, low_rest),
            (couple_high, up_rest),
            (killing, jnp.ones_like(low_rest)),
        )
    ):
        for x in range(planes):
            rows[n, x * knots : x * knots + segments, :] = value[x]
            rows[n, x * knots + segments : (x + 1) * knots, :] = other[x]
    for x in range(planes):
        rows[3, x * knots : x * knots + segments, :] = high_gain[x]
        rows[4, x * knots : x * knots + segments, :] = sum_first[x]

    def row(n, s):
        return rows[n, pl.ds(s, planes, stride=knots), :]

    top = knots - 1
    one_row = jnp.ones((planes, across), jnp.float32)
    d, d_b = one_row, one_row
    inv_s, gain_s, ratio_s = [], [], []
    inv_sb, gain_sb = [None] * top, [None] * top
    for s in range(top):
        e = row(2, s) + row(0, s) * d
        inverse = reciprocal(row(1, s) + e)
        inv_s.append(inverse)
        gain_s.append(row(0, s) * inverse)
        ratio_s.append(row(1, s) * inverse)
        d = e * inverse
        back = top - 1 - s
        e_b = row(2, back) + row(1, back) * d_b
        inverse_b = reciprocal(row(0, back) + e_b)
        inv_sb[back] = inverse_b
        gain_sb[back] = row(1, back) * inverse_b
        d_b = e_b * inverse_b
        inner[0, s] = inv_s[s]
        inner[1, s] = gain_s[s]
        inner[2, s] = ratio_s[s]
    run = row(0, top)
    low_total = one_row
    sum_top = one_row
    rows[5, pl.ds(top, planes, stride=knots), :] = one_row
    for s in reversed(range(top)):
        weight = run * inv_s[s]
        rows[5, pl.ds(s, planes, stride=knots), :] = weight
        sum_top = sum_top + weight * row(2, s)
        run = run * gain_s[s]
        low_total = low_total * gain_s[s]
    run = row(3, 0)
    high_total = one_row
    sum_bottom = row(4, 0)
    rows[6, pl.ds(top, planes, stride=knots), :] = jnp.zeros_like(one_row)
    for s in range(top):
        weight = run * inv_sb[s]
        rows[6, pl.ds(s, planes, stride=knots), :] = weight
        sum_bottom = sum_bottom + weight * row(2, s)
        run = run * gain_sb[s]
        high_total = high_total * ratio_s[s]
    coef = (
        row(0, top) * low_total,
        sum_top,
        row(1, top),
        sum_bottom,
        row(3, 0) * high_total,
    )
    for n, value in enumerate(coef):
        coefs[n * planes : (n + 1) * planes, :] = value
    for n in range(2):
        for x in range(planes):
            ends[n, x] = rows[5 + n, x * knots : (x + 1) * knots, :]
    wait_all(outgoing)


def deposit_kernel(got, from_above, from_below, cells, ends, coefs, *refs):
    (deposit_hbm, swept, prefix, ratio, reduced, sums) = refs[6:12]
    (work, rhs, inv, first, lower, upper) = refs[12:18]
    (field, total, lefts, rights, columns, edges, in_sems, sems) = refs[18:]
    incoming = copies_of(refs[:6], refs[12:18], in_sems)
    start_all(incoming)
    components, planes, height, across = rhs.shape
    steps = inv.shape[0] + 1
    last = steps - 1
    knots = ends.shape[2]
    rest = knots - segments
    chunks = got.shape[2]
    parts = height // lanes
    shift = across.bit_length() - 1
    lines = components * planes
    kind = jnp.bfloat16 if max(height, across) <= 256 else jnp.float32

    total[...] = jnp.zeros_like(total)
    for p in range(parts):
        part = slice(p * lines, (p + 1) * lines)
        columns[p, pl.ds(0, lines, stride=2), :] = from_above[part, :]
        columns[p, pl.ds(1, lines, stride=2), :] = from_below[part, :]
        edges[p * lanes : (p + 1) * lanes, :] = diffusion_number * columns[p].T

    tile = 16
    base = lax.broadcasted_iota(jnp.int32, (tile, lanes), 0)
    height_ids = [(base + n * tile).astype(jnp.float32).astype(kind) for n in range(height // tile)]
    across_ids = height_ids[: across // tile]
    lane = lane_iota((1, lanes))
    one = jnp.ones((tile, lanes), jnp.bfloat16)
    none = jnp.zeros((tile, lanes), jnp.bfloat16)

    def spread(row, to):
        return jnp.broadcast_to(row, (tile, lanes)).astype(to)

    def build(n, half):
        for g in range(group):
            word = work[(n + 1) * group + g]
            ident = (word >> count_bits) & ((1 << (plane_bit - count_bits)) - 1)
            live = word & ((1 << count_bits) - 1)
            there = slice(g * lanes, (g + 1) * lanes)
            sender, chunk = lax.div(ident, chunks), lax.rem(ident, chunks)
            x = word >> plane_bit
            cell = cells[sender, chunk, pl.ds(x, 1), :]
            up = jnp.where(lane < live, cell >> shift, -1).astype(jnp.float32)
            side = (cell & (across - 1)).astype(jnp.float32)
            up, side = spread(up, kind), spread(side, kind)
            for i, ids in enumerate(height_ids):
                lefts[half][i * tile : (i + 1) * tile, there] = jnp.where(up == ids, one, none)
            masks = [side == ids for ids in across_ids]
            for c in range(components):
                force = got[sender, c, chunk, pl.ds(x, 1), :]
                rest_of = force - force.astype(jnp.bfloat16).astype(jnp.float32)
                for m, value in enumerate((force, rest_of)):
                    value = spread(value, jnp.bfloat16)
                    start = (m * components + c) * across
                    for i, mask in enumerate(masks):
                        place = slice(start + i * tile, start + (i + 1) * tile)
                        rights[half][place, there] = jnp.where(mask, value, none)

    def add(n, half):
        total[work[(n + 1) * group] >> plane_bit] += lax.dot_general(
            lefts[half][...],
            rights[half][...],
            (((1,), (1,)), ((), ())),
            preferred_element_type=jnp.float32,
        )

    def two_steps(n, carry):
        add(2 * n, 0)
        build(2 * n + 1, 1)
        add(2 * n + 1, 1)
        build(2 * n + 2, 0)
        return carry

    incoming[0].wait()
    build(0, 0)
    count = work[0]
    lax.fori_loop(0, lax.div(count, 2), two_steps, 0)

    @pl.when(lax.rem(count, 2) == 1)
    def _():
        add(count - 1, 0)

    wait_all(incoming[1:])

    wide = lane_iota((lanes, across))
    border = (wide == 0) | (wide == across - 1)

    def place(x):
        return [
            pltpu.make_async_copy(field.at[c, x], deposit_hbm.at[c, x], sems.at[c, x])
            for c in range(components)
        ]

    def combine(x, carry):
        for c in range(components):
            for p in range(parts):
                part = slice(p * lanes, (p + 1) * lanes)
                high = total[x, part, c * across : (c + 1) * across]
                low = total[x, part, (components + c) * across : (components + c + 1) * across]
                value = high + low
                field[c, x, part, :] = value.astype(jnp.bfloat16)
                edge = pltpu.roll(edges[part, :], lanes - 1 - 2 * (c * planes + x), 1)
                rhs[c, x, part, :] = rhs[c, x, part, :] + value + jnp.where(border, edge, 0.0)
        start_all(place(x))
        return carry

    lax.fori_loop(0, planes, combine, 0)
    copies = sums.shape[0]
    for n in range(copies):
        sums[n, 2 * lines : 2 * lines + coefs.shape[0], :] = coefs[...]

    zero = jnp.zeros((components, planes, segments, across), jnp.float32)

    def of_step(t):
        return rhs[:, :, pl.ds(t, segments, stride=steps), :]

    def forward(t, carry):
        value, start, run, before = carry
        force = of_step(t)
        low, inverse = lower[:, pl.ds(t, segments, stride=steps), :], inv[t]
        value = force + (low * before)[None] * value
        swept[t] = inverse[None] * value
        run = run * (low * inverse)
        prefix[t] = run
        ratio[t] = upper[:, pl.ds(t, segments, stride=steps), :] * inverse
        return value, start + first[t][None] * force, run, inverse

    one = jnp.ones((planes, segments, across), jnp.float32)
    value, start, _, inverse = lax.fori_loop(0, last, forward, (zero, zero, one, one), unroll=3)
    value = inverse[None] * value
    segment = lax.broadcasted_iota(jnp.int32, zero.shape, 2)
    after = jnp.where(segment == segments - 1, 0.0, jnp.roll(start, -1, axis=2))
    low_sep, up_sep = ends[2, :, :segments, :], ends[3, :, :segments, :]
    value = of_step(last) + low_sep[None] * value + up_sep[None] * after
    others = rhs[:, :, height - rest :, :]
    at_top = ends[0, :, :segments, :][None] * value + ends[0, :, segments:, :][None] * others
    at_bottom = ends[1, :, :segments, :][None] * value + ends[1, :, segments:, :][None] * others
    at_bottom = at_bottom + jnp.where(segment == 0, start, 0.0)
    for c in range(components):
        for x in range(planes):
            k = c * planes + x
            reduced[k * knots : k * knots + segments, :] = value[c, x]
            reduced[k * knots + segments : (k + 1) * knots, :] = others[c, x]
            top = jnp.sum(at_top[c, x], 0, keepdims=True)
            bottom = jnp.sum(at_bottom[c, x], 0, keepdims=True)
            for n in range(copies):
                sums[n, k : k + 1, :] = top
                sums[n, lines + k : lines + k + 1, :] = bottom

    for x in range(planes):
        wait_all(place(x))


def finish_kernel(sums, inner, reduced, swept, ratio, prefix, *refs):
    walls = sums.shape[0]
    out_hbm, tops, after, before, out, sems = refs
    components, planes, height, across = out.shape
    steps = swept.shape[0] + 1
    last = steps - 1
    lines = components * planes
    knots = inner.shape[1] + 1
    rest = knots - segments
    me = lax.axis_index("wall")

    def coef(k, n):
        start = 2 * lines + n * planes
        return sums[k, start : start + planes, :]

    def wide(value):
        return jnp.concatenate([value] * components, 0)

    d = jnp.ones((planes, across), jnp.float32)
    value = jnp.zeros((lines, across), jnp.float32)
    values, ratios = [], []
    for k in range(walls):
        low, own, up = coef(k, 0), coef(k, 1), coef(k, 2)
        right = sums[k, :lines, :]
        if k + 1 < walls:
            high = up * coef(k + 1, 4)
            killing = own + up * coef(k + 1, 3)
            right = right + wide(up) * sums[k + 1, lines : 2 * lines, :]
        else:
            high = jnp.zeros_like(up)
            killing = own + up
        e = killing + low * d
        inverse = reciprocal(high + e)
        d = e * inverse
        value = (right + wide(low) * value) * wide(inverse)
        values.append(value)
        ratios.append(wide(high * inverse))
    tops[0] = jnp.zeros((lines, across), jnp.float32)
    tops[walls] = values[-1]
    for k in reversed(range(walls - 1)):
        values[k] = values[k] + ratios[k] * values[k + 1]
        tops[k + 1] = values[k]

    def row(s):
        return pl.ds(s, lines, stride=knots)

    run = tops[me]
    before[row(0), :] = run
    found = []
    for s in range(knots - 1):
        run = reduced[row(s), :] * wide(inner[0, s]) + wide(inner[1, s]) * run
        found.append(run)
    run = tops[me + 1]
    after[row(knots - 1), :] = run
    for s in reversed(range(knots - 1)):
        run = found[s] + wide(inner[2, s]) * run
        after[row(s), :] = run
        if s + 1 < segments:
            before[row(s + 1), :] = run

    def put(c, x, t, value):
        out[c, x, pl.ds(t, segments, stride=steps), :] = value

    copies = []
    half = planes // 2 if planes % 2 == 0 else planes
    for start in range(0, planes, half):
        part = [(c, x) for c in range(components) for x in range(start, start + half)]
        bottoms, starts = [], []
        for c, x in part:
            base = (c * planes + x) * knots
            bottoms.append(before[base : base + segments, :])
            starts.append(after[base : base + segments, :])
            out[c, x, height - rest :, :] = after[base + segments : base + knots, :]
            put(c, x, last, starts[-1])

        def backward(n, values):
            t = last - 1 - n
            found = []
            for (c, x), value, bottom in zip(part, values, bottoms):
                value = (swept[t, c, x] + prefix[t, x] * bottom) + ratio[t, x] * value
                put(c, x, t, value)
                found.append(value)
            return tuple(found)

        lax.fori_loop(0, last, backward, tuple(starts), unroll=5)
        for here in part:
            copy = pltpu.make_async_copy(out.at[here], out_hbm.at[here], sems.at[here])
            copy.start()
            copies.append(copy)
    wait_all(copies)


def shifted(block, axis, distance):
    length = lax.axis_size(axis)
    route = [(i, (i + distance) % length) for i in range(length)]
    return lax.ppermute(block, axis, route)


def local(velocity, lower_weight, upper_weight, forces, cells, counts):
    components, planes, height, across = velocity.shape
    receivers, capacity = forces.shape[3], forces.shape[5]
    senders = cells.shape[2]
    walls = lax.axis_size("wall")
    lines = components * planes
    chunks = capacity // lanes
    counts_shape = (planes, senders)
    forces = forces.reshape(components, receivers, planes, capacity)
    cells = cells.reshape(senders, planes, capacity)
    counts = counts.reshape(senders, planes).T

    def hbm(*arrays):
        return [pltpu.with_memory_space_constraint(array, pltpu.HBM) for array in arrays]

    work_shape = (planes * (senders * chunks + group) + 4 * group,)
    send, lower_near, upper_near, velocity_near, work = call(
        load_kernel,
        (
            pltpu.HBM((receivers, components, planes, capacity), jnp.float32),
            f32(*lower_weight.shape),
            f32(*upper_weight.shape),
            f32(*velocity.shape),
            jax.ShapeDtypeStruct(work_shape, jnp.int32),
        ),
        (in_hbm, *[in_vmem] * 4),
        [in_hbm] * 5,
        [
            scratch(*forces.shape),
            pltpu.SMEM(counts_shape, jnp.int32),
            pltpu.SMEM(work_shape, jnp.int32),
            pltpu.SemaphoreType.DMA((3 * components + 4,)),
        ],
        4,
        1 << 16,
    )(*hbm(forces, velocity, lower_weight, upper_weight, counts))
    got = lax.all_to_all(send, "span", 0, 0, tiled=True)
    got = got.reshape(senders, components, planes, chunks, lanes).transpose(0, 1, 3, 2, 4)
    cells = cells.reshape(senders, planes, chunks, lanes).transpose(0, 2, 1, 3)
    edge_shape = (lines * height // lanes, lanes)
    first_column, last_column = call(
        edge_kernel,
        (f32(*edge_shape), f32(*edge_shape)),
        (in_vmem, in_vmem),
        [in_vmem],
        [scratch(height, across), scratch(height // lanes, lanes, lanes)],
        4,
        1 << 20,
    )(velocity_near)
    from_above = shifted(first_column, "span", -1)
    from_below = shifted(last_column, "span", 1)

    steps = height // segments - 1
    knots = height - segments * steps + segments
    step_shape = (steps - 1, planes, segments, across)
    staged = [velocity.shape, step_shape, step_shape]
    prepared = call(
        prepare_kernel,
        (
            f32(3, knots - 1, planes, across),
            f32(4, planes, knots, across),
            f32(5 * planes, across),
            *[pltpu.HBM(shape, jnp.float32) for shape in staged],
        ),
        [in_vmem] * 3 + [in_hbm] * 3,
        [in_vmem] * 3,
        [
            *[scratch(*shape) for shape in staged],
            scratch(*step_shape),
            scratch(*step_shape),
            scratch(7, planes * knots, across),
            pltpu.SemaphoreType.DMA((3,)),
        ],
        12,
        1 << 24,
    )(velocity_near, lower_near, upper_near)
    (inner, ends, coefs, rhs_start, inv, first) = prepared

    sum_rows = -(-(2 * lines + 5 * planes) // 8) * 8
    wide = 2 * components * across
    deposit, swept, prefix, ratio, reduced, sums = call(
        deposit_kernel,
        (
            jax.ShapeDtypeStruct(velocity.shape, jnp.bfloat16),
            f32(steps - 1, components, planes, segments, across),
            f32(*step_shape),
            f32(*step_shape),
            f32(lines * knots, across),
            f32(walls, sum_rows, across),
        ),
        (in_hbm, *[in_vmem] * 5),
        [in_vmem] * 7 + [in_hbm] * 5,
        [
            pltpu.SMEM(work_shape, jnp.int32),
            *[scratch(*shape) for shape in staged],
            scratch(*lower_weight.shape),
            scratch(*upper_weight.shape),
            pltpu.VMEM(velocity.shape, jnp.bfloat16),
            scratch(planes, height, wide),
            [pltpu.VMEM((height, group * lanes), jnp.bfloat16)] * 2,
            [pltpu.VMEM((wide, group * lanes), jnp.bfloat16)] * 2,
            scratch(height // lanes, lanes, lanes),
            scratch(height, lanes),
            pltpu.SemaphoreType.DMA((6,)),
            pltpu.SemaphoreType.DMA((components, planes)),
        ],
        24,
        1 << 32,
    )(
        got,
        from_above,
        from_below,
        cells,
        ends,
        coefs,
        work,
        *hbm(rhs_start, inv, first, lower_weight, upper_weight),
    )
    all_sums = lax.all_to_all(sums, "wall", 0, 0, tiled=True)

    velocity_next = call(
        finish_kernel,
        f32(*velocity.shape),
        in_hbm,
        [in_vmem] * 6,
        [
            scratch(walls + 1, lines, across),
            scratch(lines * knots, across),
            scratch(lines * knots, across),
            scratch(*velocity.shape),
            pltpu.SemaphoreType.DMA((components, planes)),
        ],
        8,
        1 << 22,
    )(all_sums, inner, reduced, swept, ratio, prefix)
    return (velocity_next, deposit)


def solution(mesh):
    placed = (
        P(None, None, "wall", "span"),
        P(None, "wall", "span"),
        P(None, "wall", "span"),
        P(None, "wall", "span", None, None, None),
        P("wall", "span", None, None, None),
        P("wall", "span", None, None),
    )
    return jax.shard_map(
        local,
        mesh=mesh,
        in_specs=placed,
        out_specs=(P(None, None, "wall", "span"), P(None, None, "wall", "span")),
        check_vma=False,
    )
```

profile of v0, /device:TPU:0, one launch (start us, length us, event | category | flops | bytes accessed | tf_op | source)
XLA Modules:
  0.0 40.6 jit_solution(11251280699694276154)
XLA Ops:
  0.6 2.0 %shard_map.77 = (f32[8,3,4,768]{3,2,1,0:T(4,128)}, f32[4,256,128]{2,1,0:T(8,128)S(1)}, f32[4,256,128]{2,1,0:T(8,128)S(1)}, f32[3,4,256,128]{3,2,1,0:T(8,128)S(1)}, s32[256]{0:T(256)S(1)}) custom-call(f32[3,8,4,768]{3,2,1,0:T(4,128)} %bitcast.12, f32[3,4,256,128]{3,2,1,0:T(8,128)} %velocity.1, f32[4,256,128]{2,1,0:T(8,128)} %refs_4_.1, ...), custom_call_target="tpu_custom_call" | custom-call | flops 65536 | bytes 4194304 | tf_op jit(solution)/shard_map/pallas_call | solution.py:556
  2.6 5.2 %all-to-all-start = ((f32[8,3,4,768]{3,2,1,0:T(4,128)}), f32[8,3,4,768]{3,2,1,0:T(4,128)S(1)}, u32[]{:S(2)}, u32[]{:S(2)}) async-start(f32[8,3,4,768]{3,2,1,0:T(4,128)} %get-tuple-element.21), calls=%async_computation | async-start | bytes 589824 | tf_op jit(solution)/shard_map/all_to_all | solution.py:576
  7.8 0.5 %shard_map.78 = (f32[24,128]{1,0:T(8,128)S(1)}, f32[24,128]{1,0:T(8,128)S(1)}) custom-call(f32[3,4,256,128]{3,2,1,0:T(8,128)S(1)} %get-tuple-element.22.velocity), custom_call_target="tpu_custom_call" | custom-call | flops 1048576 | bytes 4194304 | tf_op jit(solution)/shard_map/pallas_call | solution.py:580
  8.3 0.0 copy-start
  8.3 2.7 %collective-permute-start = (f32[24,128]{1,0:T(8,128)S(1)}, f32[24,128]{1,0:T(8,128)S(1)}, u32[]{:S(2)}, u32[]{:S(2)}) collective-permute-start(f32[24,128]{1,0:T(8,128)S(1)} %get-tuple-element.23), channel_id=1, source_target_pairs={{0,7},{1,0},{2,1},{3,2},{4,3},{5,4},{6,5},{7,6},{8,15},{9,8},{10,9... | collective-permute-start | bytes 36872 | tf_op jit(solution)/shard_map/ppermute | solution.py:537
  11.1 0.0 collective-permute-start.1
  11.1 3.5 %shard_map.79 = (f32[3,15,4,128]{3,2,1,0:T(4,128)S(1)}, f32[4,4,16,128]{3,2,1,0:T(8,128)S(1)}, f32[20,128]{1,0:T(8,128)S(1)}, f32[3,4,256,128]{3,2,1,0:T(8,128)}...) custom-call(f32[3,4,256,128]{3,2,1,0:T(8,128)S(1)} %get-tuple-element.22.velocity, ...), custom_call_target="tpu_custom_call" | custom-call | flops 16777216 | bytes 4194304 | tf_op jit(solution)/shard_map/pallas_call | solution.py:596
  14.6 0.0 collective-permute-done.from_above
  14.6 0.7 %collective-permute-done.1.from_below = f32[24,128]{1,0:T(8,128)S(1)} collective-permute-done((f32[24,128]{1,0:T(8,128)S(1)}, f32[24,128]{1,0:T(8,128)S(1)}, u32[]{:S(2)}, u32[]{:S(2)}) %collective-permute-start.1) | collective-permute-done | bytes 12320 | tf_op jit(solution)/shard_map/ppermute | solution.py:537
  15.3 0.0 all-to-all-done
  15.3 0.0 copy-done
  15.3 7.5 %shard_map.80 = (bf16[3,4,256,128]{3,2,1,0:T(8,128)(2,1)}, f32[30,3,4,8,128]{4,3,2,1,0:T(8,128)S(1)}, f32[30,4,8,128]{3,2,1,0:T(8,128)S(1)}, f32[30,4,8,128]{3,2...) custom-call(f32[8,3,6,4,128]{4,3,2,1,0:T(4,128)S(1)} %bitcast.10, ...), custom_call_target="tpu_custom_call" | custom-call | flops 4294967296 | bytes 4194304 | tf_op jit(solution)/shard_map/pallas_call | solution.py:620
  22.8 16.3 %all_to_all.10.sums = f32[4,48,128]{2,1,0:T(8,128)S(1)} all-to-all(f32[4,48,128]{2,1,0:T(8,128)S(1)} %get-tuple-element.33), channel_id=1, replica_groups=mesh['wall'=4,'span'=8] {'wall'}, dimensions={0} | all-to-all | bytes 196608 | tf_op jit(solution)/shard_map/all_to_all | solution.py:658
  39.0 1.5 %shard_map.81 = f32[3,4,256,128]{3,2,1,0:T(8,128)} custom-call(f32[4,48,128]{2,1,0:T(8,128)S(1)} %all_to_all.10.sums, f32[3,15,4,128]{3,2,1,0:T(4,128)S(1)} %get-tuple-element.34.inner, f32[192,128]{1,0:T(8,128)S(1)} %get-tuple-element.35.reduced, f32[30,3,4,8,128]{4,3,2,1,0:T(8,128)S(1)} %get-tuple-element.36.swept, ...), custom_call_target="tpu_custom_call" | custom-call | flops 4194304 | bytes 4194304 | tf_op jit(solution)/shard_map/pallas_call | solution.py:660
Async XLA Ops:
  2.6 12.7 %all-to-all-start = ((f32[8,3,4,768]{3,2,1,0:T(4,128)}), f32[8,3,4,768]{3,2,1,0:T(4,128)S(1)}, u32[]{:S(2)}, u32[]{:S(2)}) async-start(f32[8,3,4,768]{3,2,1,0:T(4,128)} %get-tuple-element.21), calls=%async_computation | async-start | bytes 589824 | tf_op jit(solution)/shard_map/all_to_all | solution.py:576
  8.3 7.0 %copy-start = (s32[1,1,8,4,768]{4,3,2,1,0:T(4,128)S(1)}, s32[1,1,8,4,768]{4,3,2,1,0:T(4,128)}, u32[]{:S(2)}) copy-start(s32[1,1,8,4,768]{4,3,2,1,0:T(4,128)} %param.10) | copy-start | bytes 294916
  8.3 6.2 %collective-permute-start = (f32[24,128]{1,0:T(8,128)S(1)}, f32[24,128]{1,0:T(8,128)S(1)}, u32[]{:S(2)}, u32[]{:S(2)}) collective-permute-start(f32[24,128]{1,0:T(8,128)S(1)} %get-tuple-element.23), channel_id=1, source_target_pairs={{0,7},{1,0},{2,1},{3,2},{4,3},{5,4},{6,5},{7,6},{8,15},{9,8},{10,9... | collective-permute-start | bytes 36872 | tf_op jit(solution)/shard_map/ppermute | solution.py:537
  11.1 4.2 %collective-permute-start.1 = (f32[24,128]{1,0:T(8,128)S(1)}, f32[24,128]{1,0:T(8,128)S(1)}, u32[]{:S(2)}, u32[]{:S(2)}) collective-permute-start(f32[24,128]{1,0:T(8,128)S(1)} %get-tuple-element.24), channel_id=1, source_target_pairs={{0,1},{1,2},{2,3},{3,4},{4,5},{5,6},{6,7},{7,0},{8,9},{9,10},{10,1... | collective-permute-start | bytes 36872 | tf_op jit(solution)/shard_map/ppermute | solution.py:537
where the time goes:
time: 40.4 us; the launch traced here: 40.6 us
  blocking collectives  16.3 us (40%)
  Pallas kernels  15 us (37%)
  starting transfers between devices  7.91 us (20%)
  waiting for transfers between devices  0.71 us (2%)
  between operations  0.68 us (2%)
    all_to_all x1, blocking collectives, local(): all_sums = lax.all_to_all(sums, 'wall', 0, 0, tiled=True)  16.3 us
    pallas_call x1, Pallas kernels, local(): call(deposit_kernel, (jax.ShapeDtypeStruct(velocity.shape, jnp.bfloat16),...  7.47 us
    all_to_all x1, starting transfers between devices, local(): got = lax.all_to_all(send, 'span', 0, 0, tiled=True)  5.18 us
    pallas_call x1, Pallas kernels, local(): call(prepare_kernel, (f32(3, knots - 1, planes, across), f32(4, planes, k...  3.49 us
    ppermute x2, starting transfers between devices, shifted(): return lax.ppermute(block, axis, route)  2.73 us
    pallas_call x1, Pallas kernels, local(): call(load_kernel, (pltpu.HBM((receivers, components, planes, capacity), j...  1.99 us
    pallas_call x1, Pallas kernels, local(): call(finish_kernel, f32(*velocity.shape), in_hbm, [in_vmem] * 6, [scratch...  1.54 us
  transfers between devices with their start and end apart: 3, of which 1 were waited for; matrix products, arithmetic and copies ran while one was open for 0% of the time, Pallas kernels for 10%

commit v1 on v0

--- a/solution.py
+++ b/solution.py
@@ -393,9 +393,7 @@
         return carry
 
     lax.fori_loop(0, planes, combine, 0)
-    copies = sums.shape[0]
-    for n in range(copies):
-        sums[n, 2 * lines : 2 * lines + coefs.shape[0], :] = coefs[...]
+    sums[2 * lines : 2 * lines + coefs.shape[0], :] = coefs[...]
 
     zero = jnp.zeros((components, planes, segments, across), jnp.float32)
 
@@ -414,7 +412,7 @@
         return value, start + first[t][None] * force, run, inverse
 
     one = jnp.ones((planes, segments, across), jnp.float32)
-    value, start, _, inverse = lax.fori_loop(0, last, forward, (zero, zero, one, one), unroll=3)
+    value, start, _, inverse = lax.fori_loop(0, last, forward, (zero, zero, one, one), unroll=6)
     value = inverse[None] * value
     segment = lax.broadcasted_iota(jnp.int32, zero.shape, 2)
     after = jnp.where(segment == segments - 1, 0.0, jnp.roll(start, -1, axis=2))
@@ -431,17 +429,17 @@
             reduced[k * knots + segments : (k + 1) * knots, :] = others[c, x]
             top = jnp.sum(at_top[c, x], 0, keepdims=True)
             bottom = jnp.sum(at_bottom[c, x], 0, keepdims=True)
-            for n in range(copies):
-                sums[n, k : k + 1, :] = top
-                sums[n, lines + k : lines + k + 1, :] = bottom
+            sums[k : k + 1, :] = top
+            sums[lines + k : lines + k + 1, :] = bottom
 
     for x in range(planes):
         wait_all(place(x))
 
 
-def finish_kernel(sums, inner, reduced, swept, ratio, prefix, *refs):
-    walls = sums.shape[0]
-    out_hbm, tops, after, before, out, sems = refs
+def finish_kernel(inner, reduced, swept, ratio, prefix, *refs):
+    walls = len(refs) - 7
+    received = refs[:walls]
+    out_hbm, sums, tops, after, before, out, sems = refs[walls:]
     components, planes, height, across = out.shape
     steps = swept.shape[0] + 1
     last = steps - 1
@@ -449,6 +447,8 @@
     knots = inner.shape[1] + 1
     rest = knots - segments
     me = lax.axis_index("wall")
+    for n in range(walls):
+        sums[lax.rem(me + walls - n, walls)] = received[n][...]
 
     def coef(k, n):
         start = 2 * lines + n * planes
@@ -523,7 +523,7 @@
                 found.append(value)
             return tuple(found)
 
-        lax.fori_loop(0, last, backward, tuple(starts), unroll=5)
+        lax.fori_loop(0, last, backward, tuple(starts), unroll=10)
         for here in part:
             copy = pltpu.make_async_copy(out.at[here], out_hbm.at[here], sems.at[here])
             copy.start()
@@ -535,6 +535,10 @@
     length = lax.axis_size(axis)
     route = [(i, (i + distance) % length) for i in range(length)]
     return lax.ppermute(block, axis, route)
+
+
+def everyone(block, axis):
+    return [block] + [shifted(block, axis, n) for n in range(1, lax.axis_size(axis))]
 
 
 def local(velocity, lower_weight, upper_weight, forces, cells, counts):
@@ -625,7 +629,7 @@
             f32(*step_shape),
             f32(*step_shape),
             f32(lines * knots, across),
-            f32(walls, sum_rows, across),
+            f32(sum_rows, across),
         ),
         (in_hbm, *[in_vmem] * 5),
         [in_vmem] * 7 + [in_hbm] * 5,
@@ -655,14 +659,15 @@
         work,
         *hbm(rhs_start, inv, first, lower_weight, upper_weight),
     )
-    all_sums = lax.all_to_all(sums, "wall", 0, 0, tiled=True)
+    all_sums = everyone(sums, "wall")
 
     velocity_next = call(
         finish_kernel,
         f32(*velocity.shape),
         in_hbm,
-        [in_vmem] * 6,
+        [in_vmem] * (5 + walls),
         [
+            scratch(walls, sum_rows, across),
             scratch(walls + 1, lines, across),
             scratch(lines * knots, across),
             scratch(lines * knots, across),
@@ -671,7 +676,7 @@
         ],
         8,
         1 << 22,
-    )(all_sums, inner, reduced, swept, ratio, prefix)
+    )(inner, reduced, swept, ratio, prefix, *all_sums)
     return (velocity_next, deposit)
 
 

time: 40.4 us -> 38.4 us (0.950); the launches traced: 40.6 us -> 38 us
  blocking collectives: 16.3 us -> 0 us
  starting transfers between devices: 7.91 us -> 15.9 us
  waiting for transfers between devices: 0.71 us -> 6.34 us
    all_to_all x1 -> x0, blocking collectives: 16.3 us -> none  [local(): all_sums = lax.all_to_all(sums, 'wall', 0, 0, tiled=True)]
    ppermute x2 -> x5, starting transfers between devices: 2.73 us -> 10.7 us  [shifted(): return lax.ppermute(block, axis, route)]
    ppermute x2 -> x5, waiting for transfers between devices: 0.71 us -> 6.34 us  [shifted(): return lax.ppermute(block, axis, route)]
  transfers between devices with their start and end apart: 3 -> 6, of which waited for: 1 -> 4; matrix products, arithmetic and copies ran while one was open for 0% -> 0% of each run, Pallas kernels for 10% -> 11%
where the time goes in v1:
time: 38.4 us; the launch traced here: 38 us
  starting transfers between devices  15.9 us (41%)
  Pallas kernels  15.1 us (39%)
  waiting for transfers between devices  6.34 us (17%)
  between operations  0.68 us (2%)
    ppermute x5, starting transfers between devices, shifted(): return lax.ppermute(block, axis, route)  10.7 us
    pallas_call x1, Pallas kernels, local(): call(deposit_kernel, (jax.ShapeDtypeStruct(velocity.shape, jnp.bfloat16),...  7.52 us
    ppermute x5, waiting for transfers between devices, shifted(): return lax.ppermute(block, axis, route)  6.34 us
    all_to_all x1, starting transfers between devices, local(): got = lax.all_to_all(send, 'span', 0, 0, tiled=True)  5.18 us
    pallas_call x1, Pallas kernels, local(): call(prepare_kernel, (f32(3, knots - 1, planes, across), f32(4, planes, k...  3.48 us
    pallas_call x1, Pallas kernels, local(): call(load_kernel, (pltpu.HBM((receivers, components, planes, capacity), j...  1.99 us
    pallas_call x1, Pallas kernels, local(): call(finish_kernel, f32(*velocity.shape), in_hbm, [in_vmem] * (5 + walls)...  1.55 us
  transfers between devices with their start and end apart: 6, of which 4 were waited for; matrix products, arithmetic and copies ran while one was open for 0% of the time, Pallas kernels for 11%

profile of v1, /device:TPU:0, one launch (start us, length us, event | category | flops | bytes accessed | tf_op | source)
XLA Modules:
  0.0 38.0 jit_solution(17850482760402314967)
XLA Ops:
  0.6 2.0 %shard_map.77 = (f32[8,3,4,768]{3,2,1,0:T(4,128)}, f32[4,256,128]{2,1,0:T(8,128)S(1)}, f32[4,256,128]{2,1,0:T(8,128)S(1)}, f32[3,4,256,128]{3,2,1,0:T(8,128)S(1)}, s32[256]{0:T(256)S(1)}) custom-call(f32[3,8,4,768]{3,2,1,0:T(4,128)} %bitcast.12, f32[3,4,256,128]{3,2,1,0:T(8,128)} %velocity.1, f32[4,256,128]{2,1,0:T(8,128)} %refs_4_.1, ...), custom_call_target="tpu_custom_call" | custom-call | flops 65536 | bytes 4194304 | tf_op jit(solution)/shard_map/pallas_call | solution.py:560
  2.6 5.2 %all-to-all-start = ((f32[8,3,4,768]{3,2,1,0:T(4,128)}), f32[8,3,4,768]{3,2,1,0:T(4,128)S(1)}, u32[]{:S(2)}, u32[]{:S(2)}) async-start(f32[8,3,4,768]{3,2,1,0:T(4,128)} %get-tuple-element.25), calls=%async_computation | async-start | bytes 589824 | tf_op jit(solution)/shard_map/all_to_all | solution.py:580
  7.8 0.5 %shard_map.79 = (f32[24,128]{1,0:T(8,128)S(1)}, f32[24,128]{1,0:T(8,128)S(1)}) custom-call(f32[3,4,256,128]{3,2,1,0:T(8,128)S(1)} %get-tuple-element.21.velocity), custom_call_target="tpu_custom_call" | custom-call | flops 1048576 | bytes 4194304 | tf_op jit(solution)/shard_map/pallas_call | solution.py:584
  8.3 0.0 copy-start
  8.3 2.7 %collective-permute-start = (f32[24,128]{1,0:T(8,128)S(1)}, f32[24,128]{1,0:T(8,128)S(1)}, u32[]{:S(2)}, u32[]{:S(2)}) collective-permute-start(f32[24,128]{1,0:T(8,128)S(1)} %get-tuple-element.26), channel_id=1, source_target_pairs={{0,7},{1,0},{2,1},{3,2},{4,3},{5,4},{6,5},{7,6},{8,15},{9,8},{10,9... | collective-permute-start | bytes 36872 | tf_op jit(solution)/shard_map/ppermute | solution.py:537
  11.1 0.0 collective-permute-start.1
  11.1 3.5 %shard_map.78 = (f32[3,15,4,128]{3,2,1,0:T(4,128)S(1)}, f32[4,4,16,128]{3,2,1,0:T(8,128)S(1)}, f32[20,128]{1,0:T(8,128)S(1)}, f32[3,4,256,128]{3,2,1,0:T(8,128)}...) custom-call(f32[3,4,256,128]{3,2,1,0:T(8,128)S(1)} %get-tuple-element.21.velocity, ...), custom_call_target="tpu_custom_call" | custom-call | flops 16777216 | bytes 4194304 | tf_op jit(solution)/shard_map/pallas_call | solution.py:600
  14.6 0.0 collective-permute-done.from_above
  14.6 0.7 %collective-permute-done.1.from_below = f32[24,128]{1,0:T(8,128)S(1)} collective-permute-done((f32[24,128]{1,0:T(8,128)S(1)}, f32[24,128]{1,0:T(8,128)S(1)}, u32[]{:S(2)}, u32[]{:S(2)}) %collective-permute-start.1) | collective-permute-done | bytes 12320 | tf_op jit(solution)/shard_map/ppermute | solution.py:537
  15.3 0.0 all-to-all-done
  15.3 0.0 copy-done
  15.3 7.5 %shard_map.80 = (bf16[3,4,256,128]{3,2,1,0:T(8,128)(2,1)}, f32[30,3,4,8,128]{4,3,2,1,0:T(8,128)S(1)}, f32[30,4,8,128]{3,2,1,0:T(8,128)S(1)}, f32[30,4,8,128]{3,2...) custom-call(f32[8,3,6,4,128]{4,3,2,1,0:T(4,128)S(1)} %bitcast.10, ...), custom_call_target="tpu_custom_call" | custom-call | flops 4294967296 | bytes 4194304 | tf_op jit(solution)/shard_map/pallas_call | solution.py:624
  22.8 6.1 %collective-permute-start.4 = (f32[48,128]{1,0:T(8,128)S(1)}, f32[48,128]{1,0:T(8,128)S(1)}, u32[]{:S(2)}, u32[]{:S(2)}) collective-permute-start(f32[48,128]{1,0:T(8,128)S(1)} %get-tuple-element.38.refs_0_), channel_id=1, source_target_pairs={{0,24},{8,0},{16,8},{24,16},{1,25},{9,1},{17,9},{25,17},{2,26},{10... | collective-permute-start | bytes 73736 | tf_op jit(solution)/shard_map/ppermute | solution.py:537
  28.9 1.9 %collective-permute-start.3 = (f32[48,128]{1,0:T(8,128)S(1)}, f32[48,128]{1,0:T(8,128)S(1)}, u32[]{:S(2)}, u32[]{:S(2)}) collective-permute-start(f32[48,128]{1,0:T(8,128)S(1)} %get-tuple-element.38.refs_0_), channel_id=1, source_target_pairs={{0,16},{8,24},{16,0},{24,8},{1,17},{9,25},{17,1},{25,9},{2,18},{10... | collective-permute-start | bytes 73736 | tf_op jit(solution)/shard_map/ppermute | solution.py:537
  30.8 0.0 collective-permute-start.2
  30.8 0.3 collective-permute-done.4.refs_3_
  31.2 2.9 %collective-permute-done.3.refs_2_ = f32[48,128]{1,0:T(8,128)S(1)} collective-permute-done((f32[48,128]{1,0:T(8,128)S(1)}, f32[48,128]{1,0:T(8,128)S(1)}, u32[]{:S(2)}, u32[]{:S(2)}) %collective-permute-start.3) | collective-permute-done | bytes 24608 | tf_op jit(solution)/shard_map/ppermute | solution.py:537
  34.1 2.4 %collective-permute-done.2.refs_1_ = f32[48,128]{1,0:T(8,128)S(1)} collective-permute-done((f32[48,128]{1,0:T(8,128)S(1)}, f32[48,128]{1,0:T(8,128)S(1)}, u32[]{:S(2)}, u32[]{:S(2)}) %collective-permute-start.2) | collective-permute-done | bytes 24608 | tf_op jit(solution)/shard_map/ppermute | solution.py:537
  36.5 1.5 %shard_map.81 = f32[3,4,256,128]{3,2,1,0:T(8,128)} custom-call(f32[3,15,4,128]{3,2,1,0:T(4,128)S(1)} %get-tuple-element.24.inner, f32[192,128]{1,0:T(8,128)S(1)} %get-tuple-element.34.reduced, f32[30,3,4,8,128]{4,3,2,1,0:T(8,128)S(1)} %get-tuple-element.35.swept, f32[30,4,8,128]{3,2,1,0:T(8,128)S(1)} %get-tuple-element.36.ratio, ...), custom_call_target="tpu_custom_call" | custom-call | flops 4194304 | bytes 4194304 | tf_op jit(solution)/shard_map/pallas_call | solution.py:664
Async XLA Ops:
  2.6 12.7 %all-to-all-start = ((f32[8,3,4,768]{3,2,1,0:T(4,128)}), f32[8,3,4,768]{3,2,1,0:T(4,128)S(1)}, u32[]{:S(2)}, u32[]{:S(2)}) async-start(f32[8,3,4,768]{3,2,1,0:T(4,128)} %get-tuple-element.25), calls=%async_computation | async-start | bytes 589824 | tf_op jit(solution)/shard_map/all_to_all | solution.py:580
  8.3 7.0 %copy-start = (s32[1,1,8,4,768]{4,3,2,1,0:T(4,128)S(1)}, s32[1,1,8,4,768]{4,3,2,1,0:T(4,128)}, u32[]{:S(2)}) copy-start(s32[1,1,8,4,768]{4,3,2,1,0:T(4,128)} %param.10) | copy-start | bytes 294916
  8.3 6.2 %collective-permute-start = (f32[24,128]{1,0:T(8,128)S(1)}, f32[24,128]{1,0:T(8,128)S(1)}, u32[]{:S(2)}, u32[]{:S(2)}) collective-permute-start(f32[24,128]{1,0:T(8,128)S(1)} %get-tuple-element.26), channel_id=1, source_target_pairs={{0,7},{1,0},{2,1},{3,2},{4,3},{5,4},{6,5},{7,6},{8,15},{9,8},{10,9... | collective-permute-start | bytes 36872 | tf_op jit(solution)/shard_map/ppermute | solution.py:537
  11.1 4.2 %collective-permute-start.1 = (f32[24,128]{1,0:T(8,128)S(1)}, f32[24,128]{1,0:T(8,128)S(1)}, u32[]{:S(2)}, u32[]{:S(2)}) collective-permute-start(f32[24,128]{1,0:T(8,128)S(1)} %get-tuple-element.27), channel_id=1, source_target_pairs={{0,1},{1,2},{2,3},{3,4},{4,5},{5,6},{6,7},{7,0},{8,9},{9,10},{10,1... | collective-permute-start | bytes 36872 | tf_op jit(solution)/shard_map/ppermute | solution.py:537
  22.8 8.3 %collective-permute-start.4 = (f32[48,128]{1,0:T(8,128)S(1)}, f32[48,128]{1,0:T(8,128)S(1)}, u32[]{:S(2)}, u32[]{:S(2)}) collective-permute-start(f32[48,128]{1,0:T(8,128)S(1)} %get-tuple-element.38.refs_0_), channel_id=1, source_target_pairs={{0,24},{8,0},{16,8},{24,16},{1,25},{9,1},{17,9},{25,17},{2,26},{10... | collective-permute-start | bytes 73736 | tf_op jit(solution)/shard_map/ppermute | solution.py:537
  28.9 5.1 %collective-permute-start.3 = (f32[48,128]{1,0:T(8,128)S(1)}, f32[48,128]{1,0:T(8,128)S(1)}, u32[]{:S(2)}, u32[]{:S(2)}) collective-permute-start(f32[48,128]{1,0:T(8,128)S(1)} %get-tuple-element.38.refs_0_), channel_id=1, source_target_pairs={{0,16},{8,24},{16,0},{24,8},{1,17},{9,25},{17,1},{25,9},{2,18},{10... | collective-permute-start | bytes 73736 | tf_op jit(solution)/shard_map/ppermute | solution.py:537
  30.8 5.6 %collective-permute-start.2 = (f32[48,128]{1,0:T(8,128)S(1)}, f32[48,128]{1,0:T(8,128)S(1)}, u32[]{:S(2)}, u32[]{:S(2)}) collective-permute-start(f32[48,128]{1,0:T(8,128)S(1)} %get-tuple-element.38.refs_0_), channel_id=1, source_target_pairs={{0,8},{8,16},{16,24},{24,0},{1,9},{9,17},{17,25},{25,1},{2,10},{10... | collective-permute-start | bytes 73736 | tf_op jit(solution)/shard_map/ppermute | solution.py:537
